TPU v7x, 32 devices: a whole 2x2x4 slice. The times are simulated.
32 devices in a mesh: band: 4 (over z), grid: 8 (over y, x, core).
Axes of the slice: x: 2, y: 2, z: 4, core: 2. Of those that a mesh axis runs over, the one named last changes fastest.
Arguments:
- orbitals: float32 [16, 96, 9216], P('band', 'grid'), may hold values from -6 to 6
- pair_mask: int32 [16, 4], P('band'), may hold values 0 or 1
- cycle_step: int32 [], replicated, may hold values from 1 to 3
Outputs:
- exchange_field: float32 [16, 96, 9216], P('band', 'grid')
- projection: float32 [16, 4], P('band')
All inputs are finite; a program needn't handle non-finite values. No bound on the sum of `pair_mask` on one device may be relied on, other than what follows from the above.
Results may differ from a plain program's by a relative error of at most 0.0003.
Values sent between devices are 32-bit elements; how exact they have to be, the bound alone decides.
No kernel may reach another device: no remote copies, remote signals or barrier semaphores. Data moves between devices by JAX's collectives and lax.ppermute only.
A program may use at most 192 MiB of HBM per device.

v0:
```python
import functools
import math

import jax
import jax.numpy as jnp
import ml_dtypes
import numpy as np
from jax import lax
from jax.experimental import pallas as pl
from jax.experimental.pallas import tpu as pltpu
from jax.sharding import PartitionSpec as P

NX = 96
NY = 96
NZ = 96
LANES = 128


box_length = 16.0
highest = lax.Precision.HIGHEST


def passed_along(block, axis, distance):
    devices = range(lax.axis_size(axis))
    route = [((i - distance) % len(devices), i) for i in devices]
    return lax.ppermute(block, axis, route)


def hartley_table(length):
    index = jnp.arange(length, dtype=jnp.int32)
    product = index[:, None] * index[None, :] % length
    angle = product.astype(jnp.float32) * (2.0 * math.pi / length)
    return jnp.cos(angle) + jnp.sin(angle)


def folded(index, length):
    return jnp.where(index * 2 >= length, index - length, index).astype(jnp.float32)


def across_planes(field, table_y, table_z):
    count = field.shape[0]
    planes = field.shape[1]
    shaped = field.reshape(count * planes * NY, NZ)
    shaped = jnp.matmul(shaped, table_z, precision=highest)
    shaped = shaped.reshape(count * planes, NY, NZ)
    shaped = jnp.matmul(table_y, shaped, precision=highest)
    return shaped.reshape(count, planes, NY * NZ)


def slab_plan(orbitals, pair_mask, cycle_step):
    orbit_count = orbitals.shape[0]
    planes = orbitals.shape[1]
    grid_count = lax.axis_size("grid")
    slab_rows = NY // grid_count

    def one_hop(turn, block):
        return passed_along(block, "band", 1)

    visiting = lax.fori_loop(0, cycle_step, one_hop, orbitals)
    table_x = hartley_table(NX)
    table_y = hartley_table(NY)
    table_z = hartley_table(NZ)
    row_index = lax.axis_index("grid") * slab_rows + jnp.arange(slab_rows, dtype=jnp.int32)
    freq_x = folded(jnp.arange(NX, dtype=jnp.int32), NX)
    freq_y = folded(row_index, NY)
    freq_z = folded(jnp.arange(NZ, dtype=jnp.int32), NZ)
    squares = freq_x[:, None, None] ** 2 + freq_y[None, :, None] ** 2 + freq_z[None, None, :] ** 2
    coulomb = box_length * box_length / math.pi / (NX * NY * NZ)
    kernel = jnp.where(squares > 0.5, coulomb / jnp.maximum(squares, 1.0), jnp.float32(0.0))
    kernel = kernel.reshape(NX, slab_rows * NZ)

    def solve_items(spectra):
        along = jnp.matmul(table_x, spectra, precision=highest) * kernel
        along = jnp.matmul(table_x, along, precision=highest)
        return lax.all_to_all(along, "grid", split_axis=1, concat_axis=2, tiled=True)

    mask_float = pair_mask.astype(jnp.float32).reshape(
        orbit_count // orbit_count, orbit_count, orbit_count
    )
    own_rows = orbitals.reshape(orbit_count // orbit_count, orbit_count, planes, NY * NZ)

    def one_group(carry, inputs):
        rows, weights = inputs
        density = (rows[:, None] * visiting[None]).reshape(
            orbit_count * orbit_count, planes, NY * NZ
        )
        spectra = across_planes(density, table_y, table_z)
        potential = solve_items(
            lax.all_to_all(spectra, "grid", split_axis=2, concat_axis=1, tiled=True)
        )
        potential = across_planes(potential, table_y, table_z)
        potential = potential.reshape(orbit_count, orbit_count, planes, NY * NZ)
        field = -jnp.einsum("aj,ajxr->axr", weights, potential * visiting[None], precision=highest)
        return (carry, field)

    start_carry = jnp.zeros((), jnp.float32)
    _, fields = lax.scan(one_group, start_carry, (own_rows, mask_float))
    exchange_field = fields.reshape(orbit_count, planes, NY * NZ)
    local_terms = jnp.einsum("axr,cxr->ac", orbitals, exchange_field, precision=highest) / (
        NX * NY * NZ
    )
    projection = lax.psum(local_terms, "grid")
    return (exchange_field, projection)


SLABS = 8
GROUP = 4
SLAB_PLANES = NX // SLABS
COLS = NY * NZ // LANES
SLAB_ROWS = SLAB_PLANES * COLS
OCTETS = NY // 8
PITCH = NX + 8
UNROLL = (6, 4, 4)
PAIR_VMEM = 36 << 20

bf16 = jnp.bfloat16
f32 = jnp.float32
in_vmem = pl.BlockSpec(memory_space=pltpu.VMEM)
in_smem = pl.BlockSpec(memory_space=pltpu.SMEM)


def high_low(table):
    high = table.astype(ml_dtypes.bfloat16)
    return high, (table - high.astype(np.float64)).astype(ml_dtypes.bfloat16)


def cas_table(length):
    index = np.arange(length)
    angle = (index[:, None] * index[None, :] % length) * (2.0 * np.pi / length)
    return np.cos(angle) + np.sin(angle)


def lane_table(table):
    high, low = high_low(table)
    out = np.zeros((2 * LANES, 2 * LANES), high.dtype)
    for row in (0, LANES):
        out[row : row + NZ, :NZ] = high
        out[row : row + NZ, LANES : LANES + NZ] = low
    return out


def row_table(table):
    high, low = high_low(table)
    return np.concatenate([np.concatenate([high, high], 1), np.concatenate([low, low], 1)], 0)


def plane_order(device):
    return np.concatenate([np.arange(SLAB_PLANES) + SLAB_PLANES * (device ^ k) for k in range(SLABS)])


def split(value):
    high = value.astype(bf16)
    return high, (value - high.astype(f32)).astype(bf16)


def product(left, right):
    return lax.dot_general(left, right, (((1,), (0,)), ((), ())), preferred_element_type=f32)


def along_lanes(value, table):
    both = product(jnp.concatenate(split(value), axis=1), table)
    return both[:, :LANES] + both[:, LANES:]


def along_rows(table, value):
    both = product(table, jnp.concatenate(split(value), axis=0))
    half = both.shape[0] // 2
    return both[:half] + both[half:]


def prepare_kernel(place, block, *refs):
    outs, natural = refs[:-1], refs[-1]
    me = place[0]

    def two_columns(step, carry):
        for a in range(GROUP):
            pair = [block[:, a, pl.ds(pl.multiple_of((2 * step + i) * LANES, LANES), LANES)] for i in range(2)]
            natural[a, pl.ds(pl.multiple_of(2 * SLAB_PLANES * step, 8), 2 * SLAB_PLANES), :] = jnp.concatenate(pair, 0)
        return carry

    lax.fori_loop(0, COLS // 2, two_columns, 0, unroll=2)
    for k in range(GROUP):
        outs[min(k, 2)][k // 3] = natural[(me & 3) ^ k]
        outs[3 + k][0] = natural[((me >> 2) * 2) ^ k]


def prepare(place, block):
    slabs = [jax.ShapeDtypeStruct((count, SLAB_ROWS, LANES), f32) for count in (1, 1, 2, 1, 1, 1, 1)]
    return pl.pallas_call(
        prepare_kernel,
        out_shape=slabs,
        in_specs=[in_smem, in_vmem],
        out_specs=[in_vmem] * 7,
        scratch_shapes=[pltpu.VMEM((GROUP, SLAB_ROWS, LANES), f32)],
        compiler_params=pltpu.CompilerParams(vmem_limit_bytes=32 << 20),
        cost_estimate=pl.CostEstimate(flops=0, bytes_accessed=6 << 20, transcendentals=0),
    )(place, block)


def tables_kernel(place, lanes_in, rows_in, forward_in, back_in, table_z, table_y, table_x, table_back, coulomb, sems):
    me = place[0]
    copies = [
        pltpu.make_async_copy(source, target, sems.at[i])
        for i, (source, target) in enumerate(
            ((lanes_in, table_z), (rows_in, table_y), (forward_in.at[me], table_x), (back_in.at[me], table_back))
        )
    ]
    for copy in copies:
        copy.start()
    scale = box_length * box_length / math.pi / (NX * NY * NZ)
    row = lax.broadcasted_iota(jnp.int32, (NY, LANES), 0)
    lane = lax.broadcasted_iota(jnp.int32, (NY, LANES), 1)
    plane = jnp.minimum(row, NY - row) ** 2 + jnp.minimum(lane, NZ - lane) ** 2
    plane = plane.astype(f32)

    def one_plane(x, carry):
        squares = plane + (x * x).astype(f32)
        coulomb[x] = jnp.where((squares > 0.5) & (lane < NZ), scale / jnp.maximum(squares, 1.0), 0.0)
        return carry

    lax.fori_loop(0, NX // 2 + 1, one_plane, 0)
    for copy in copies:
        copy.wait()


def make_tables(place, tables):
    return pl.pallas_call(
        tables_kernel,
        out_shape=[
            jax.ShapeDtypeStruct(tables[0].shape, bf16),
            *[jax.ShapeDtypeStruct(tables[1].shape, bf16)] * 3,
            jax.ShapeDtypeStruct((NX // 2 + 1, NY, LANES), f32),
        ],
        in_specs=[in_smem] + [pl.BlockSpec(memory_space=pl.ANY)] * 4,
        out_specs=[in_vmem] * 5,
        scratch_shapes=[pltpu.SemaphoreType.DMA((4,))],
        compiler_params=pltpu.CompilerParams(vmem_limit_bytes=16 << 20),
        cost_estimate=pl.CostEstimate(flops=0, bytes_accessed=1 << 20, transcendentals=0),
    )(place, *tables)


OWN_PLACES = ((0, 0), (4, 0), (1, 0), (4, 1), (2, 0), (4, 2), (3, 0), (5, 1))
VISITING_PLACES = (
    ((0, 0), (1, 0), (2, 0), (3, 0), (0, 1), (1, 1), (2, 1), (3, 1)),
    tuple((k, 0) for k in range(SLABS)),
)


def pair_kernel(turn, place, mask, *refs):
    places = VISITING_PLACES[turn]
    count = 1 + max(i for i, _ in places)
    own_refs, vis_refs, refs = refs[:6], refs[6 : 6 + count], refs[6 + count :]
    own_slabs = [own_refs[i].at[j] for i, j in OWN_PLACES]
    vis_slabs = [vis_refs[i].at[j] for i, j in places]
    table_z, table_y, table_x, table_back, coulomb, *refs = refs
    if turn:
        before, *refs = refs
        outs, refs = refs[:SLABS], refs[SLABS:]
    else:
        out, *refs = refs
    vis, spectrum = refs
    me = place[0]
    weight = -mask[me & 3, (me >> 2) * 2 + turn].astype(f32)

    def rows_of(step):
        return pl.ds(pl.multiple_of(2 * SLAB_PLANES * step, 8), 2 * SLAB_PLANES)

    def plane_of(y):
        return pl.ds(pl.multiple_of(y * PITCH, 8), NX)

    def columns_of(slabs, step):
        pieces = [slab[rows_of(step), :] for slab in slabs]
        return [
            jnp.concatenate([piece[:SLAB_PLANES] for piece in pieces], axis=0),
            jnp.concatenate([piece[SLAB_PLANES:] for piece in pieces], axis=0),
        ]

    def lane_index():
        return lax.broadcasted_iota(jnp.int32, (NX, LANES), 1)

    def forward(octet, carry):
        lane = lane_index()
        densities = []
        for i in range(3):
            step = 3 * octet + i
            pair = columns_of(vis_slabs, step)
            for j in range(2):
                vis[2 * step + j] = pair[j]
            densities += [a * b for a, b in zip(columns_of(own_slabs, step), pair)]
        for q in range(2):
            first, second, third = densities[3 * q : 3 * q + 3]
            rows = [
                first,
                pltpu.roll(jnp.where(lane >= 96, first, second), 32, 1),
                pltpu.roll(jnp.where(lane >= 64, second, third), 64, 1),
                pltpu.roll(third, 96, 1),
            ]
            done = along_lanes(jnp.concatenate(rows, axis=0), table_z[...])
            for j in range(2):
                both = [done[(2 * j + i) * NX : (2 * j + i + 1) * NX] for i in range(2)]
                both = along_rows(table_x[...], jnp.concatenate(both, axis=1))
                at = 8 * octet + 4 * q + 2 * j
                spectrum[plane_of(at), :] = both[:, :LANES]
                spectrum[plane_of(at + 1), :] = both[:, LANES:]
        return carry

    lax.fori_loop(0, OCTETS, forward, 0, unroll=UNROLL[0])

    def middle(step, carry):
        base = pl.multiple_of(8 * step, 8)
        for j in range(4):
            at = [base + 2 * j, base + 2 * j + 1]
            lines = [pl.ds(i, NY, stride=PITCH) for i in at]
            both = along_rows(table_y[...], jnp.concatenate([spectrum[line, :] for line in lines], axis=1))
            both = both * jnp.concatenate([coulomb[jnp.minimum(i, NX - i)] for i in at], axis=1)
            both = along_rows(table_y[...], both)
            for i, line in enumerate(lines):
                spectrum[line, :] = both[:, i * LANES : (i + 1) * LANES]
        return carry

    lax.fori_loop(0, NX // 8, middle, 0, unroll=UNROLL[1])

    def back(octet, carry):
        lane = lane_index()
        values = []
        for q in range(2):
            rows = []
            for j in range(2):
                at = 8 * octet + 4 * q + 2 * j
                both = along_rows(table_back[...], jnp.concatenate([spectrum[plane_of(at + i), :] for i in range(2)], axis=1))
                rows += [both[:, :LANES], both[:, LANES:]]
            done = along_lanes(jnp.concatenate(rows, axis=0), table_z[...])
            first, second, third, fourth = [done[NX * i : NX * (i + 1)] for i in range(4)]
            second = pltpu.roll(second, 96, 1)
            third = pltpu.roll(third, 64, 1)
            fourth = pltpu.roll(fourth, 32, 1)
            columns = (
                jnp.where(lane < 96, first, second),
                jnp.where(lane < 64, second, third),
                jnp.where(lane < 32, third, fourth),
            )
            for i in range(3):
                at = 6 * octet + 3 * q + i
                value = weight * (columns[i] * vis[at])
                if turn:
                    values.append(before[at] + value)
                else:
                    out[at] = value
        if turn:
            for i in range(3):
                even, odd = values[2 * i : 2 * i + 2]
                for k in range(SLABS):
                    cut = slice(SLAB_PLANES * k, SLAB_PLANES * (k + 1))
                    outs[k][rows_of(3 * octet + i), :] = jnp.concatenate([even[cut], odd[cut]], axis=0)
        return carry

    lax.fori_loop(0, OCTETS, back, 0, unroll=UNROLL[2])


def pair_step(turn, place, mask, own, visiting, tables, before=None):
    extra = [] if before is None else [before]
    whole = jax.ShapeDtypeStruct((COLS, NX, LANES), f32)
    slab = jax.ShapeDtypeStruct((SLAB_ROWS, LANES), f32)
    return pl.pallas_call(
        functools.partial(pair_kernel, turn),
        out_shape=[slab] * SLABS if turn else whole,
        in_specs=[in_smem] * 2 + [in_vmem] * (len(own) + len(visiting) + 5 + len(extra)),
        out_specs=[in_vmem] * SLABS if turn else in_vmem,
        scratch_shapes=[
            pltpu.VMEM((COLS, NX, LANES), f32),
            pltpu.VMEM((NY * PITCH, LANES), f32),
        ],
        compiler_params=pltpu.CompilerParams(vmem_limit_bytes=PAIR_VMEM),
        cost_estimate=pl.CostEstimate(flops=0, bytes_accessed=1 << 20, transcendentals=0),
    )(place, mask, *own, *visiting, *tables, *extra)


def gram_kernel(place, *refs):
    parts, refs = refs[:SLABS], refs[SLABS:]
    own, refs = refs[:3], refs[3:]
    natural, gram = refs
    me = place[0] & 3
    for k in range(GROUP):
        natural[me ^ k] = parts[k][...] + parts[k + GROUP][...]
    for a in range(GROUP):
        for c in range(GROUP):
            terms = own[min(a, 2)][a // 3] * natural[me ^ c]
            terms = jnp.sum(terms.reshape(SLAB_ROWS // 8, 8, LANES), axis=0)
            gram[(me ^ a) * GROUP + (me ^ c)] = jnp.sum(terms, axis=0, keepdims=True)


def layout_kernel(natural, out):
    def two_columns(step, carry):
        rows = pl.ds(pl.multiple_of(2 * SLAB_PLANES * step, 8), 2 * SLAB_PLANES)
        for a in range(GROUP):
            pair = natural[a, rows, :]
            for i in range(2):
                lanes = pl.ds(pl.multiple_of((2 * step + i) * LANES, LANES), LANES)
                out[:, a, lanes] = pair[SLAB_PLANES * i : SLAB_PLANES * (i + 1)]
        return carry

    lax.fori_loop(0, COLS // 2, two_columns, 0, unroll=2)


def finish(place, parts, own):
    natural, gram = pl.pallas_call(
        gram_kernel,
        out_shape=[
            jax.ShapeDtypeStruct((GROUP, SLAB_ROWS, LANES), f32),
            jax.ShapeDtypeStruct((GROUP * GROUP, 1, LANES), f32),
        ],
        in_specs=[in_smem] + [in_vmem] * (SLABS + 3),
        out_specs=[in_vmem] * 2,
        compiler_params=pltpu.CompilerParams(vmem_limit_bytes=32 << 20),
        cost_estimate=pl.CostEstimate(flops=0, bytes_accessed=8 << 20, transcendentals=0),
    )(place, *parts, *own)
    field = pl.pallas_call(
        layout_kernel,
        out_shape=jax.ShapeDtypeStruct((SLAB_PLANES, GROUP, NY * NZ), f32),
        in_specs=[in_vmem],
        out_specs=in_vmem,
        compiler_params=pltpu.CompilerParams(vmem_limit_bytes=32 << 20),
        cost_estimate=pl.CostEstimate(flops=0, bytes_accessed=8 << 20, transcendentals=0),
    )(natural)
    gram = jnp.sum(gram.reshape(GROUP, GROUP, LANES), axis=2) / (NX * NY * NZ)
    gram = gram + to_partner(gram, 1)
    gram = (gram + to_partner(gram, 2)) + (to_partner(gram, 4) + to_partner(gram, 6))
    return field, gram


def to_partner(block, flip):
    return lax.ppermute(block, "grid", [(i, i ^ flip) for i in range(SLABS)])


def to_group(block, distance, flip):
    bands = lax.axis_size("band")
    route = [(b * SLABS + i, (b + distance) % bands * SLABS + (i ^ flip)) for b in range(bands) for i in range(SLABS)]
    return lax.ppermute(block, ("band", "grid"), route)


def after(value, *others):
    return lax.optimization_barrier((value, *others))[0]


def pair_plan(orbitals, pair_mask, cycle_step):
    me = lax.axis_index("grid")
    place = me.astype(jnp.int32).reshape(1)
    cas = cas_table(NX)
    forward_x = jnp.asarray(np.stack([row_table(cas[:, plane_order(d)]) for d in range(SLABS)]))
    back_x = jnp.asarray(np.stack([row_table(cas[plane_order(d), :]) for d in range(SLABS)]))
    fixed = jnp.asarray(lane_table(cas)), jnp.asarray(row_table(cas)), forward_x, back_x
    slabs = prepare(place, jnp.transpose(orbitals, (1, 0, 2)))

    bands = lax.axis_size("band")

    def with_distance(distance, slabs, pair_mask, place, fixed):
        own_out, vis_out = slabs[:3], slabs[3:]
        own_y = to_partner(own_out[0], 4)
        across = to_group(vis_out[2], distance, 4)
        home = to_group(vis_out[0], distance, 0)
        own_next = to_partner(own_out[1], 4)
        own_x = to_partner(own_out[2], 2)
        near = min(distance, bands - distance) == 1
        first = jnp.concatenate([after(home, own_x, own_y), across])
        first_x = to_partner(first, 2)
        across = to_group(after(vis_out[3], first), distance, 4)
        home = to_group(after(vis_out[1], first if near else across), distance, 0)
        tables = make_tables(after(place, first), fixed)
        if near:
            own_far = to_partner(after(own_x, across, own_next, *tables), 4)
            home_x, across_x = to_partner(home, 2), to_partner(across, 2)
            ready, last = home, home_x
        else:
            own_far = to_partner(after(own_x, own_next, *tables), 4)
            ready = last = across
        crossing = jnp.concatenate([after(own_out[1], ready if not near else first), own_x[1:], own_next])
        crossed, far_crossed = to_partner(crossing, 1), to_partner(after(own_far, last), 1)
        first_core, beside_core = to_partner(after(first, ready), 1), to_partner(after(first_x, ready), 1)
        own = [own_out[0], own_x, own_y, own_far, crossed, far_crossed]
        visiting = [first, first_core, first_x, beside_core]
        total = pair_step(0, place, pair_mask, own, visiting, tables)
        if not near:
            home_x, across_x = to_partner(after(home, total), 2), to_partner(across, 2)
        cores = [to_partner(slab, 1) for slab in (home, home_x, across)]
        cores.append(to_partner(after(across_x, total), 1))
        visiting = [home, cores[0], home_x, cores[1], across, cores[2], across_x, cores[3]]
        parts = pair_step(1, place, pair_mask, own, visiting, tables, total)
        parts = [parts[0]] + [to_partner(parts[k], k) for k in range(1, SLABS)]
        return finish(place, parts, own_out)

    field, gram = lax.switch(
        cycle_step - 1,
        [functools.partial(with_distance, distance) for distance in range(1, bands)],
        slabs,
        pair_mask,
        place,
        fixed,
    )
    return jnp.transpose(field, (1, 0, 2)), gram


def shards(orbitals, pair_mask, cycle_step):
    if lax.axis_size("grid") == SLABS and orbitals.shape[0] == GROUP:
        return pair_plan(orbitals, pair_mask, cycle_step)
    return slab_plan(orbitals, pair_mask, cycle_step)


def solution(mesh):
    return jax.shard_map(
        shards,
        mesh=mesh,
        in_specs=(P("band", "grid", None), P("band", None), P()),
        out_specs=(P("band", "grid", None), P("band", None)),
        check_vma=False,
    )
```

profile of v0, /device:TPU:0, one launch (start us, length us, event | category | flops | bytes accessed | tf_op | source)
XLA Modules:
  0.0 148.4 jit_solution(12737103136296198207)
XLA Ops:
  1.3 1.5 copy-done
  2.8 1.5 %shard_map.86 = (f32[1,864,128]{2,1,0:T(8,128)S(1)}, f32[1,864,128]{2,1,0:T(8,128)S(1)}, f32[2,864,128]{2,1,0:T(8,128)S(1)}, f32[1,864,128]{2,1,0:T(8,128)S(1)},...) custom-call(s32[1]{0:T(128)} %bitcast.place, f32[12,4,9216]{2,1,0:T(4,128)S(1)} %bitcast.3), custom_call_target="tpu_custom_call" | custom-call | bytes 6291456 | tf_op jit(solution)/shard_map/pallas_call | solution.py:189
  4.3 142.8 %conditional.1 = (f32[12,4,9216]{2,1,0:T(4,128)S(1)}, f32[4,4]{1,0:T(4,128)S(1)}) conditional(s32[]{:T(128)} %clamp.3, (f32[2,864,128]{2,1,0:T(8,128)S(1)}, f32[1,864,128]{2,1,0:T(8,128)S(1)}, f32[1,864,128]{2,1,0:T(8,128)S(1)}, f32[1,864,128]{2,1,0:T(8,128)S(1)}, f32[1,864,128]{2,1,0:T(8,128)S(1)}, ...), branch_computations={%region_0.0_spmd, %region_2.0_spmd, %region_4.0_spmd} | conditional | flops 665664 | bytes 85699616 | solution.py:491
  4.4 3.0 %collective-permute-start = (f32[2,864,128]{2,1,0:T(8,128)S(1)}, f32[2,864,128]{2,1,0:T(8,128)S(1)}, u32[]{:S(2)}, u32[]{:S(2)}) collective-permute-start(f32[2,864,128]{2,1,0:T(8,128)S(1)} %get-tuple-element.81.refs_10_), channel_id=1, source_target_pairs={{0,2},{1,3},{2,0},{3,1},{4,6},{5,7},{6,4},{7,5},{8,10},{9,11},{10,... | collective-permute-start | bytes 2654216 | tf_op jit(solution)/shard_map/cond/branch_0_fun/ppermute | solution.py:432
  7.4 1.6 %collective-permute-start.2 = (f32[1,864,128]{2,1,0:T(8,128)S(1)}, f32[1,864,128]{2,1,0:T(8,128)S(1)}, u32[]{:S(2)}, u32[]{:S(2)}) collective-permute-start(f32[1,864,128]{2,1,0:T(8,128)S(1)} %get-tuple-element.83), channel_id=1, source_target_pairs={{0,8},{1,9},{2,10},{3,11},{4,12},{5,13},{6,14},{7,15},{8,16},{9,17... | collective-permute-start | bytes 1327112 | tf_op jit(solution)/shard_map/cond/branch_0_fun/ppermute | solution.py:438
  8.9 1.5 %collective-permute-start.1 = (f32[1,864,128]{2,1,0:T(8,128)S(1)}, f32[1,864,128]{2,1,0:T(8,128)S(1)}, u32[]{:S(2)}, u32[]{:S(2)}) collective-permute-start(f32[1,864,128]{2,1,0:T(8,128)S(1)} %get-tuple-element.80.refs_0_.refs_8_), channel_id=1, source_target_pairs={{0,4},{1,5},{2,6},{3,7},{4,0},{5,1},{6,2},{7,3},{8,12},{9,13},{10,... | collective-permute-start | bytes 1327112 | tf_op jit(solution)/shard_map/cond/branch_0_fun/ppermute | solution.py:432
  10.5 1.5 %collective-permute-start.3 = (f32[1,864,128]{2,1,0:T(8,128)S(1)}, f32[1,864,128]{2,1,0:T(8,128)S(1)}, u32[]{:S(2)}, u32[]{:S(2)}) collective-permute-start(f32[1,864,128]{2,1,0:T(8,128)S(1)} %get-tuple-element.85), channel_id=1, source_target_pairs={{0,12},{1,13},{2,14},{3,15},{4,8},{5,9},{6,10},{7,11},{8,20},{9,21... | collective-permute-start | bytes 1327112 | tf_op jit(solution)/shard_map/cond/branch_0_fun/ppermute | solution.py:438
  12.0 1.5 %collective-permute-start.5 = (f32[1,864,128]{2,1,0:T(8,128)S(1)}, f32[1,864,128]{2,1,0:T(8,128)S(1)}, u32[]{:S(2)}, u32[]{:S(2)}) collective-permute-start(f32[1,864,128]{2,1,0:T(8,128)S(1)} %get-tuple-element.99.refs_9_), channel_id=1, source_target_pairs={{0,4},{1,5},{2,6},{3,7},{4,0},{5,1},{6,2},{7,3},{8,12},{9,13},{10,... | collective-permute-start | bytes 1327112 | tf_op jit(solution)/shard_map/cond/branch_0_fun/ppermute | solution.py:432
  13.5 8.7 %collective-permute-done.2 = f32[1,864,128]{2,1,0:T(8,128)S(1)} collective-permute-done((f32[1,864,128]{2,1,0:T(8,128)S(1)}, f32[1,864,128]{2,1,0:T(8,128)S(1)}, u32[]{:S(2)}, u32[]{:S(2)}) %collective-permute-start.2) | collective-permute-done | bytes 442400 | tf_op jit(solution)/shard_map/cond/branch_0_fun/ppermute | solution.py:438
  22.2 9.3 %collective-permute-done.1.refs_2_ = f32[1,864,128]{2,1,0:T(8,128)S(1)} collective-permute-done((f32[1,864,128]{2,1,0:T(8,128)S(1)}, f32[1,864,128]{2,1,0:T(8,128)S(1)}, u32[]{:S(2)}, u32[]{:S(2)}) %collective-permute-start.1) | collective-permute-done | bytes 442400 | tf_op jit(solution)/shard_map/cond/branch_0_fun/ppermute | solution.py:432
  31.6 7.3 %collective-permute-start.4 = (f32[1,864,128]{2,1,0:T(8,128)S(1)}, f32[1,864,128]{2,1,0:T(8,128)S(1)}, u32[]{:S(2)}, u32[]{:S(2)}) collective-permute-start(f32[1,864,128]{2,1,0:T(8,128)S(1)} %get-tuple-element.86), channel_id=1, source_target_pairs={{0,12},{1,13},{2,14},{3,15},{4,8},{5,9},{6,10},{7,11},{8,20},{9,21... | collective-permute-start | bytes 1327112 | tf_op jit(solution)/shard_map/cond/branch_0_fun/ppermute | solution.py:438
  38.9 0.5 collective-permute-start.16
  39.5 1.6 %collective-permute-start.8 = (f32[1,864,128]{2,1,0:T(8,128)S(1)}, f32[1,864,128]{2,1,0:T(8,128)S(1)}, u32[]{:S(2)}, u32[]{:S(2)}) collective-permute-start(f32[1,864,128]{2,1,0:T(8,128)S(1)} %get-tuple-element.101), channel_id=1, source_target_pairs={{0,8},{1,9},{2,10},{3,11},{4,12},{5,13},{6,14},{7,15},{8,16},{9,17... | collective-permute-start | bytes 1327112 | tf_op jit(solution)/shard_map/cond/branch_0_fun/ppermute | solution.py:438
  41.1 1.5 %branch_0_fun.5 = (bf16[256,256]{1,0:T(8,128)(2,1)S(1)}, bf16[192,192]{1,0:T(8,128)(2,1)S(1)}, bf16[192,192]{1,0:T(8,128)(2,1)S(1)}, bf16[192,192]{1,0:T(8,128)(2,1)S(1)}, f32[49,96,128]{2,1,0:T(8,128)S(1)}) custom-call(s32[1]{0:T(128)} %get-tuple-element.88.place, bf16[256,256]{1,0:T(8,128)(2,1)S(1)} %get-tuple-element.89.lanes_in, ...), custom_call_target="tpu_custom_call" | custom-call | bytes 1048576 | tf_op jit(solution)/shard_map/cond/branch_0_fun/pallas_call | solution.py:227
  42.6 6.2 %collective-permute-done.5 = f32[1,864,128]{2,1,0:T(8,128)S(1)} collective-permute-done((f32[1,864,128]{2,1,0:T(8,128)S(1)}, f32[1,864,128]{2,1,0:T(8,128)S(1)}, u32[]{:S(2)}, u32[]{:S(2)}) %collective-permute-start.5) | collective-permute-done | bytes 442400 | tf_op jit(solution)/shard_map/cond/branch_0_fun/ppermute | solution.py:432
  48.7 1.5 %collective-permute-start.6 = (f32[2,864,128]{2,1,0:T(8,128)S(1)}, f32[2,864,128]{2,1,0:T(8,128)S(1)}, u32[]{:S(2)}, u32[]{:S(2)}) collective-permute-start(f32[2,864,128]{2,1,0:T(8,128)S(1)} %collective-permute-done.refs_1_), channel_id=1, source_target_pairs={{0,4},{1,5},{2,6},{3,7},{4,0},{5,1},{6,2},{7,3},{8,12},{9,13},{10,... | collective-permute-start | bytes 2654216 | tf_op jit(solution)/shard_map/cond/branch_0_fun/ppermute | solution.py:432
  50.4 3.0 %collective-permute-done.8.refs_6_ = f32[1,864,128]{2,1,0:T(8,128)S(1)} collective-permute-done((f32[1,864,128]{2,1,0:T(8,128)S(1)}, f32[1,864,128]{2,1,0:T(8,128)S(1)}, u32[]{:S(2)}, u32[]{:S(2)}) %collective-permute-start.8) | collective-permute-done | bytes 442400 | tf_op jit(solution)/shard_map/cond/branch_0_fun/ppermute | solution.py:438
  53.4 0.8 collective-permute-start.9
  54.2 0.5 collective-permute-start.15
  54.7 7.2 %collective-permute-done.9.refs_8_ = f32[1,864,128]{2,1,0:T(8,128)S(1)} collective-permute-done((f32[1,864,128]{2,1,0:T(8,128)S(1)}, f32[1,864,128]{2,1,0:T(8,128)S(1)}, u32[]{:S(2)}, u32[]{:S(2)}) %collective-permute-start.9) | collective-permute-done | bytes 442400 | tf_op jit(solution)/shard_map/cond/branch_0_fun/ppermute | solution.py:432
  61.9 6.1 %collective-permute-done.6.refs_3_ = f32[2,864,128]{2,1,0:T(8,128)S(1)} collective-permute-done((f32[2,864,128]{2,1,0:T(8,128)S(1)}, f32[2,864,128]{2,1,0:T(8,128)S(1)}, u32[]{:S(2)}, u32[]{:S(2)}) %collective-permute-start.6) | collective-permute-done | bytes 884768 | tf_op jit(solution)/shard_map/cond/branch_0_fun/ppermute | solution.py:432
  68.1 0.5 collective-permute-start.14
  68.6 0.2 collective-permute-start.13
  68.8 0.3 collective-permute-start.11
  69.1 0.2 collective-permute-start.12
  69.4 1.1 collective-permute-done.10.refs_5_
  70.5 11.6 %branch_0_fun.6.refs_19_ = f32[72,96,128]{2,1,0:T(8,128)S(1)} custom-call(s32[1]{0:T(128)} %get-tuple-element.88.place, s32[4,4]{1,0:T(4,128)S(1)} %get-tuple-element.79.mask, f32[1,864,128]{2,1,0:T(8,128)S(1)} %get-tuple-element.80.refs_0_.refs_8_, f32[2,864,128]{2,1,0:T(8,128)S(1)} %collective-permute-done.refs_1_, ...), custom_call_target="tpu_custom_call" | custom-call | bytes 1048576 | tf_op jit(solution)/shard_map/cond/branch_0_fun/pallas_call | solution.py:364
  82.1 0.2 collective-permute-start.18
  82.3 1.6 %collective-permute-done.18.refs_13_ = f32[1,864,128]{2,1,0:T(8,128)S(1)} collective-permute-done((f32[1,864,128]{2,1,0:T(8,128)S(1)}, f32[1,864,128]{2,1,0:T(8,128)S(1)}, u32[]{:S(2)}, u32[]{:S(2)}) %collective-permute-start.18) | collective-permute-done | bytes 442400 | tf_op jit(solution)/shard_map/cond/branch_0_fun/ppermute | solution.py:432
  83.9 11.6 %branch_0_fun.7 = (f32[864,128]{1,0:T(8,128)S(1)}, f32[864,128]{1,0:T(8,128)S(1)}, f32[864,128]{1,0:T(8,128)S(1)}, f32[864,128]{1,0:T(8,128)S(1)}, f32[864,128]{...) custom-call(s32[1]{0:T(128)} %get-tuple-element.88.place, ...), custom_call_target="tpu_custom_call" | custom-call | bytes 1048576 | tf_op jit(solution)/shard_map/cond/branch_0_fun/pallas_call | solution.py:364
  95.7 0.6 collective-permute-start.20
  96.3 1.2 collective-permute-start.21
  97.5 1.5 %collective-permute-start.22 = (f32[864,128]{1,0:T(8,128)S(1)}, f32[864,128]{1,0:T(8,128)S(1)}, u32[]{:S(2)}, u32[]{:S(2)}) collective-permute-start(f32[864,128]{1,0:T(8,128)S(1)} %get-tuple-element.110), channel_id=1, source_target_pairs={{0,4},{1,5},{2,6},{3,7},{4,0},{5,1},{6,2},{7,3},{8,12},{9,13},{10,... | collective-permute-start | bytes 1327112 | tf_op jit(solution)/shard_map/cond/branch_0_fun/ppermute | solution.py:432
  99.0 0.3 collective-permute-start.23
  99.3 1.5 %collective-permute-start.24 = (f32[864,128]{1,0:T(8,128)S(1)}, f32[864,128]{1,0:T(8,128)S(1)}, u32[]{:S(2)}, u32[]{:S(2)}) collective-permute-start(f32[864,128]{1,0:T(8,128)S(1)} %get-tuple-element.112), channel_id=1, source_target_pairs={{0,6},{1,7},{2,4},{3,5},{4,2},{5,3},{6,0},{7,1},{8,14},{9,15},{10,... | collective-permute-start | bytes 1327112 | tf_op jit(solution)/shard_map/cond/branch_0_fun/ppermute | solution.py:432
  100.7 8.0 %collective-permute-done.20.refs_2_ = f32[864,128]{1,0:T(8,128)S(1)} collective-permute-done((f32[864,128]{1,0:T(8,128)S(1)}, f32[864,128]{1,0:T(8,128)S(1)}, u32[]{:S(2)}, u32[]{:S(2)}) %collective-permute-start.20) | collective-permute-done | bytes 442400 | tf_op jit(solution)/shard_map/cond/branch_0_fun/ppermute | solution.py:432
  108.8 8.3 %collective-permute-done.21.refs_3_ = f32[864,128]{1,0:T(8,128)S(1)} collective-permute-done((f32[864,128]{1,0:T(8,128)S(1)}, f32[864,128]{1,0:T(8,128)S(1)}, u32[]{:S(2)}, u32[]{:S(2)}) %collective-permute-start.21) | collective-permute-done | bytes 442400 | tf_op jit(solution)/shard_map/cond/branch_0_fun/ppermute | solution.py:432
  117.1 20.9 %collective-permute-done.23.refs_5_ = f32[864,128]{1,0:T(8,128)S(1)} collective-permute-done((f32[864,128]{1,0:T(8,128)S(1)}, f32[864,128]{1,0:T(8,128)S(1)}, u32[]{:S(2)}, u32[]{:S(2)}) %collective-permute-start.23) | collective-permute-done | bytes 442400 | tf_op jit(solution)/shard_map/cond/branch_0_fun/ppermute | solution.py:432
  138.0 1.0 branch_0_fun.8
  139.2 0.3 collective-permute-start.26
  139.5 1.9 %branch_0_fun.9 = f32[12,4,9216]{2,1,0:T(4,128)S(1)} custom-call(f32[4,864,128]{2,1,0:T(8,128)S(1)} %get-tuple-element.114.natural), custom_call_target="tpu_custom_call" | custom-call | bytes 8388608 | tf_op jit(solution)/shard_map/cond/branch_0_fun/pallas_call | solution.py:417
  141.5 1.6 %collective-permute-start.29 = (f32[4,4]{1,0:T(4,128)S(1)}, f32[4,4]{1,0:T(4,128)S(1)}, u32[]{:S(2)}, u32[]{:S(2)}) collective-permute-start(f32[4,4]{1,0:T(4,128)S(1)} %add.25), channel_id=1, source_target_pairs={{0,6},{1,7},{2,4},{3,5},{4,2},{5,3},{6,0},{7,1},{8,14},{9,15},{10,... | collective-permute-start | bytes 200 | tf_op jit(solution)/shard_map/cond/branch_0_fun/ppermute | solution.py:432
  143.0 0.5 collective-permute-start.28
  143.6 1.5 %collective-permute-start.27 = (f32[4,4]{1,0:T(4,128)S(1)}, f32[4,4]{1,0:T(4,128)S(1)}, u32[]{:S(2)}, u32[]{:S(2)}) collective-permute-start(f32[4,4]{1,0:T(4,128)S(1)} %add.25), channel_id=1, source_target_pairs={{0,2},{1,3},{2,0},{3,1},{4,6},{5,7},{6,4},{7,5},{8,10},{9,11},{10,... | collective-permute-start | bytes 200 | tf_op jit(solution)/shard_map/cond/branch_0_fun/ppermute | solution.py:432
  145.0 1.0 collective-permute-done.29
  146.0 0.6 collective-permute-done.28
  146.6 0.5 collective-permute-done.27
  147.2 1.2 copy-done.3
  (44 shorter events, 0.9 us)
Async XLA Ops:
  0.6 3.7 %copy-start.8 = (s32[4,4]{1,0:T(4,128)S(1)}, s32[4,4]{1,0:T(4,128)}, u32[]{:S(2)}) copy-start(s32[4,4]{1,0:T(4,128)} %param.11) | copy-start | bytes 196
  1.3 1.5 copy-start
  2.8 1.5 %copy-start.1 = (bf16[8,192,192]{2,1,0:T(8,128)(2,1)S(1)}, bf16[8,192,192]{2,1,0:T(8,128)(2,1)}, u32[]{:S(2)}) copy-start(bf16[8,192,192]{2,1,0:T(8,128)(2,1)} %constant.35.clone) | copy-start | bytes 1769476
  2.8 1.5 %copy-start.2 = (bf16[8,192,192]{2,1,0:T(8,128)(2,1)S(1)}, bf16[8,192,192]{2,1,0:T(8,128)(2,1)}, u32[]{:S(2)}) copy-start(bf16[8,192,192]{2,1,0:T(8,128)(2,1)} %constant.34.clone) | copy-start | bytes 1769476
  2.8 1.5 %copy-start.4 = (bf16[256,256]{1,0:T(8,128)(2,1)S(1)}, bf16[256,256]{1,0:T(8,128)(2,1)}, u32[]{:S(2)}) copy-start(bf16[256,256]{1,0:T(8,128)(2,1)} %constant.36.clone) | copy-start | bytes 393220
  4.3 36.7 %copy-start.5 = (bf16[192,192]{1,0:T(8,128)(2,1)S(1)}, bf16[192,192]{1,0:T(8,128)(2,1)}, u32[]{:S(2)}) copy-start(bf16[192,192]{1,0:T(8,128)(2,1)} %get-tuple-element.90.rows_in) | copy-start | bytes 221188 | tf_op jit(solution)/shard_map/cond
  4.4 27.2 %collective-permute-start = (f32[2,864,128]{2,1,0:T(8,128)S(1)}, f32[2,864,128]{2,1,0:T(8,128)S(1)}, u32[]{:S(2)}, u32[]{:S(2)}) collective-permute-start(f32[2,864,128]{2,1,0:T(8,128)S(1)} %get-tuple-element.81.refs_10_), channel_id=1, source_target_pairs={{0,2},{1,3},{2,0},{3,1},{4,6},{5,7},{6,4},{7,5},{8,10},{9,11},{10,... | collective-permute-start | bytes 2654216 | tf_op jit(solution)/shard_map/cond/branch_0_fun/ppermute | solution.py:432
  7.4 14.9 %collective-permute-start.2 = (f32[1,864,128]{2,1,0:T(8,128)S(1)}, f32[1,864,128]{2,1,0:T(8,128)S(1)}, u32[]{:S(2)}, u32[]{:S(2)}) collective-permute-start(f32[1,864,128]{2,1,0:T(8,128)S(1)} %get-tuple-element.83), channel_id=1, source_target_pairs={{0,8},{1,9},{2,10},{3,11},{4,12},{5,13},{6,14},{7,15},{8,16},{9,17... | collective-permute-start | bytes 1327112 | tf_op jit(solution)/shard_map/cond/branch_0_fun/ppermute | solution.py:438
  8.9 22.6 %collective-permute-start.1 = (f32[1,864,128]{2,1,0:T(8,128)S(1)}, f32[1,864,128]{2,1,0:T(8,128)S(1)}, u32[]{:S(2)}, u32[]{:S(2)}) collective-permute-start(f32[1,864,128]{2,1,0:T(8,128)S(1)} %get-tuple-element.80.refs_0_.refs_8_), channel_id=1, source_target_pairs={{0,4},{1,5},{2,6},{3,7},{4,0},{5,1},{6,2},{7,3},{8,12},{9,13},{10,... | collective-permute-start | bytes 1327112 | tf_op jit(solution)/shard_map/cond/branch_0_fun/ppermute | solution.py:432
  10.5 21.1 %collective-permute-start.3 = (f32[1,864,128]{2,1,0:T(8,128)S(1)}, f32[1,864,128]{2,1,0:T(8,128)S(1)}, u32[]{:S(2)}, u32[]{:S(2)}) collective-permute-start(f32[1,864,128]{2,1,0:T(8,128)S(1)} %get-tuple-element.85), channel_id=1, source_target_pairs={{0,12},{1,13},{2,14},{3,15},{4,8},{5,9},{6,10},{7,11},{8,20},{9,21... | collective-permute-start | bytes 1327112 | tf_op jit(solution)/shard_map/cond/branch_0_fun/ppermute | solution.py:438
  12.0 36.7 %collective-permute-start.5 = (f32[1,864,128]{2,1,0:T(8,128)S(1)}, f32[1,864,128]{2,1,0:T(8,128)S(1)}, u32[]{:S(2)}, u32[]{:S(2)}) collective-permute-start(f32[1,864,128]{2,1,0:T(8,128)S(1)} %get-tuple-element.99.refs_9_), channel_id=1, source_target_pairs={{0,4},{1,5},{2,6},{3,7},{4,0},{5,1},{6,2},{7,3},{8,12},{9,13},{10,... | collective-permute-start | bytes 1327112 | tf_op jit(solution)/shard_map/cond/branch_0_fun/ppermute | solution.py:432
  31.6 17.1 %collective-permute-start.4 = (f32[1,864,128]{2,1,0:T(8,128)S(1)}, f32[1,864,128]{2,1,0:T(8,128)S(1)}, u32[]{:S(2)}, u32[]{:S(2)}) collective-permute-start(f32[1,864,128]{2,1,0:T(8,128)S(1)} %get-tuple-element.86), channel_id=1, source_target_pairs={{0,12},{1,13},{2,14},{3,15},{4,8},{5,9},{6,10},{7,11},{8,20},{9,21... | collective-permute-start | bytes 1327112 | tf_op jit(solution)/shard_map/cond/branch_0_fun/ppermute | solution.py:438
  38.9 15.8 %collective-permute-start.16 = (f32[2,864,128]{2,1,0:T(8,128)S(1)}, f32[2,864,128]{2,1,0:T(8,128)S(1)}, u32[]{:S(2)}, u32[]{:S(2)}) collective-permute-start(f32[2,864,128]{2,1,0:T(8,128)S(1)} %constant_dynamic-update-slice_fusion.refs_6_), channel_id=1, source_target_pairs={{0,2},{1,3},{2,0},{3,1},{4,6},{5,7},{6,4},{7,5},{8,10},{9,11},{10,... | collective-permute-start | bytes 2654216 | tf_op jit(solution)/shard_map/cond/branch_0_fun/ppermute | solution.py:432
  39.5 13.9 %collective-permute-start.8 = (f32[1,864,128]{2,1,0:T(8,128)S(1)}, f32[1,864,128]{2,1,0:T(8,128)S(1)}, u32[]{:S(2)}, u32[]{:S(2)}) collective-permute-start(f32[1,864,128]{2,1,0:T(8,128)S(1)} %get-tuple-element.101), channel_id=1, source_target_pairs={{0,8},{1,9},{2,10},{3,11},{4,12},{5,13},{6,14},{7,15},{8,16},{9,17... | collective-permute-start | bytes 1327112 | tf_op jit(solution)/shard_map/cond/branch_0_fun/ppermute | solution.py:438
  48.7 19.3 %collective-permute-start.6 = (f32[2,864,128]{2,1,0:T(8,128)S(1)}, f32[2,864,128]{2,1,0:T(8,128)S(1)}, u32[]{:S(2)}, u32[]{:S(2)}) collective-permute-start(f32[2,864,128]{2,1,0:T(8,128)S(1)} %collective-permute-done.refs_1_), channel_id=1, source_target_pairs={{0,4},{1,5},{2,6},{3,7},{4,0},{5,1},{6,2},{7,3},{8,12},{9,13},{10,... | collective-permute-start | bytes 2654216 | tf_op jit(solution)/shard_map/cond/branch_0_fun/ppermute | solution.py:432
  53.4 8.5 %collective-permute-start.9 = (f32[1,864,128]{2,1,0:T(8,128)S(1)}, f32[1,864,128]{2,1,0:T(8,128)S(1)}, u32[]{:S(2)}, u32[]{:S(2)}) collective-permute-start(f32[1,864,128]{2,1,0:T(8,128)S(1)} %collective-permute-done.8.refs_6_), channel_id=1, source_target_pairs={{0,2},{1,3},{2,0},{3,1},{4,6},{5,7},{6,4},{7,5},{8,10},{9,11},{10,... | collective-permute-start | bytes 1327112 | tf_op jit(solution)/shard_map/cond/branch_0_fun/ppermute | solution.py:432
  54.2 14.6 %collective-permute-start.7 = (f32[3,864,128]{2,1,0:T(8,128)S(1)}, f32[3,864,128]{2,1,0:T(8,128)S(1)}, u32[]{:S(2)}, u32[]{:S(2)}) collective-permute-start(f32[3,864,128]{2,1,0:T(8,128)S(1)} %pad_maximum_fusion), channel_id=1, source_target_pairs={{0,1},{1,0},{2,3},{3,2},{4,5},{5,4},{6,7},{7,6},{8,9},{9,8},{10,11... | collective-permute-start | bytes 3981320 | tf_op jit(solution)/shard_map/cond/branch_0_fun/ppermute | solution.py:432
  54.2 14.4 %collective-permute-start.15 = (f32[2,864,128]{2,1,0:T(8,128)S(1)}, f32[2,864,128]{2,1,0:T(8,128)S(1)}, u32[]{:S(2)}, u32[]{:S(2)}) collective-permute-start(f32[2,864,128]{2,1,0:T(8,128)S(1)} %constant_dynamic-update-slice_fusion.refs_6_), channel_id=1, source_target_pairs={{0,1},{1,0},{2,3},{3,2},{4,5},{5,4},{6,7},{7,6},{8,9},{9,8},{10,11... | collective-permute-start | bytes 2654216 | tf_op jit(solution)/shard_map/cond/branch_0_fun/ppermute | solution.py:432
  54.7 14.4 %collective-permute-start.17 = (f32[2,864,128]{2,1,0:T(8,128)S(1)}, f32[2,864,128]{2,1,0:T(8,128)S(1)}, u32[]{:S(2)}, u32[]{:S(2)}) collective-permute-start(f32[2,864,128]{2,1,0:T(8,128)S(1)} %collective-permute-done.16.refs_8_), channel_id=1, source_target_pairs={{0,1},{1,0},{2,3},{3,2},{4,5},{5,4},{6,7},{7,6},{8,9},{9,8},{10,11... | collective-permute-start | bytes 2654216 | tf_op jit(solution)/shard_map/cond/branch_0_fun/ppermute | solution.py:432
  68.1 2.4 %collective-permute-start.10 = (f32[2,864,128]{2,1,0:T(8,128)S(1)}, f32[2,864,128]{2,1,0:T(8,128)S(1)}, u32[]{:S(2)}, u32[]{:S(2)}) collective-permute-start(f32[2,864,128]{2,1,0:T(8,128)S(1)} %collective-permute-done.6.refs_3_), channel_id=1, source_target_pairs={{0,1},{1,0},{2,3},{3,2},{4,5},{5,4},{6,7},{7,6},{8,9},{9,8},{10,11... | collective-permute-start | bytes 2654216 | tf_op jit(solution)/shard_map/cond/branch_0_fun/ppermute | solution.py:432
  68.1 14.0 %collective-permute-start.14 = (f32[1,864,128]{2,1,0:T(8,128)S(1)}, f32[1,864,128]{2,1,0:T(8,128)S(1)}, u32[]{:S(2)}, u32[]{:S(2)}) collective-permute-start(f32[1,864,128]{2,1,0:T(8,128)S(1)} %collective-permute-done.4.refs_10_), channel_id=1, source_target_pairs={{0,2},{1,3},{2,0},{3,1},{4,6},{5,7},{6,4},{7,5},{8,10},{9,11},{10,... | collective-permute-start | bytes 1327112 | tf_op jit(solution)/shard_map/cond/branch_0_fun/ppermute | solution.py:432
  68.6 13.7 %collective-permute-start.13 = (f32[1,864,128]{2,1,0:T(8,128)S(1)}, f32[1,864,128]{2,1,0:T(8,128)S(1)}, u32[]{:S(2)}, u32[]{:S(2)}) collective-permute-start(f32[1,864,128]{2,1,0:T(8,128)S(1)} %collective-permute-done.4.refs_10_), channel_id=1, source_target_pairs={{0,1},{1,0},{2,3},{3,2},{4,5},{5,4},{6,7},{7,6},{8,9},{9,8},{10,11... | collective-permute-start | bytes 1327112 | tf_op jit(solution)/shard_map/cond/branch_0_fun/ppermute | solution.py:432
  68.8 13.4 %collective-permute-start.11 = (f32[1,864,128]{2,1,0:T(8,128)S(1)}, f32[1,864,128]{2,1,0:T(8,128)S(1)}, u32[]{:S(2)}, u32[]{:S(2)}) collective-permute-start(f32[1,864,128]{2,1,0:T(8,128)S(1)} %collective-permute-done.8.refs_6_), channel_id=1, source_target_pairs={{0,1},{1,0},{2,3},{3,2},{4,5},{5,4},{6,7},{7,6},{8,9},{9,8},{10,11... | collective-permute-start | bytes 1327112 | tf_op jit(solution)/shard_map/cond/branch_0_fun/ppermute | solution.py:432
  69.1 13.2 %collective-permute-start.12 = (f32[1,864,128]{2,1,0:T(8,128)S(1)}, f32[1,864,128]{2,1,0:T(8,128)S(1)}, u32[]{:S(2)}, u32[]{:S(2)}) collective-permute-start(f32[1,864,128]{2,1,0:T(8,128)S(1)} %collective-permute-done.9.refs_8_), channel_id=1, source_target_pairs={{0,1},{1,0},{2,3},{3,2},{4,5},{5,4},{6,7},{7,6},{8,9},{9,8},{10,11... | collective-permute-start | bytes 1327112 | tf_op jit(solution)/shard_map/cond/branch_0_fun/ppermute | solution.py:432
  82.1 1.9 %collective-permute-start.18 = (f32[1,864,128]{2,1,0:T(8,128)S(1)}, f32[1,864,128]{2,1,0:T(8,128)S(1)}, u32[]{:S(2)}, u32[]{:S(2)}) collective-permute-start(f32[1,864,128]{2,1,0:T(8,128)S(1)} %collective-permute-done.14.refs_12_), channel_id=1, source_target_pairs={{0,1},{1,0},{2,3},{3,2},{4,5},{5,4},{6,7},{7,6},{8,9},{9,8},{10,11... | collective-permute-start | bytes 1327112 | tf_op jit(solution)/shard_map/cond/branch_0_fun/ppermute | solution.py:432
  95.5 3.7 %collective-permute-start.19 = (f32[864,128]{1,0:T(8,128)S(1)}, f32[864,128]{1,0:T(8,128)S(1)}, u32[]{:S(2)}, u32[]{:S(2)}) collective-permute-start(f32[864,128]{1,0:T(8,128)S(1)} %get-tuple-element.107), channel_id=1, source_target_pairs={{0,1},{1,0},{2,3},{3,2},{4,5},{5,4},{6,7},{7,6},{8,9},{9,8},{10,11... | collective-permute-start | bytes 1327112 | tf_op jit(solution)/shard_map/cond/branch_0_fun/ppermute | solution.py:432
  95.7 13.0 %collective-permute-start.20 = (f32[864,128]{1,0:T(8,128)S(1)}, f32[864,128]{1,0:T(8,128)S(1)}, u32[]{:S(2)}, u32[]{:S(2)}) collective-permute-start(f32[864,128]{1,0:T(8,128)S(1)} %get-tuple-element.108), channel_id=1, source_target_pairs={{0,2},{1,3},{2,0},{3,1},{4,6},{5,7},{6,4},{7,5},{8,10},{9,11},{10,... | collective-permute-start | bytes 1327112 | tf_op jit(solution)/shard_map/cond/branch_0_fun/ppermute | solution.py:432
  96.3 20.8 %collective-permute-start.21 = (f32[864,128]{1,0:T(8,128)S(1)}, f32[864,128]{1,0:T(8,128)S(1)}, u32[]{:S(2)}, u32[]{:S(2)}) collective-permute-start(f32[864,128]{1,0:T(8,128)S(1)} %get-tuple-element.109), channel_id=1, source_target_pairs={{0,3},{1,2},{2,1},{3,0},{4,7},{5,6},{6,5},{7,4},{8,11},{9,10},{10,... | collective-permute-start | bytes 1327112 | tf_op jit(solution)/shard_map/cond/branch_0_fun/ppermute | solution.py:432
  97.5 19.6 %collective-permute-start.22 = (f32[864,128]{1,0:T(8,128)S(1)}, f32[864,128]{1,0:T(8,128)S(1)}, u32[]{:S(2)}, u32[]{:S(2)}) collective-permute-start(f32[864,128]{1,0:T(8,128)S(1)} %get-tuple-element.110), channel_id=1, source_target_pairs={{0,4},{1,5},{2,6},{3,7},{4,0},{5,1},{6,2},{7,3},{8,12},{9,13},{10,... | collective-permute-start | bytes 1327112 | tf_op jit(solution)/shard_map/cond/branch_0_fun/ppermute | solution.py:432
  99.0 39.0 %collective-permute-start.23 = (f32[864,128]{1,0:T(8,128)S(1)}, f32[864,128]{1,0:T(8,128)S(1)}, u32[]{:S(2)}, u32[]{:S(2)}) collective-permute-start(f32[864,128]{1,0:T(8,128)S(1)} %get-tuple-element.111), channel_id=1, source_target_pairs={{0,5},{1,4},{2,7},{3,6},{4,1},{5,0},{6,3},{7,2},{8,13},{9,12},{10,... | collective-permute-start | bytes 1327112 | tf_op jit(solution)/shard_map/cond/branch_0_fun/ppermute | solution.py:432
  99.3 38.7 %collective-permute-start.24 = (f32[864,128]{1,0:T(8,128)S(1)}, f32[864,128]{1,0:T(8,128)S(1)}, u32[]{:S(2)}, u32[]{:S(2)}) collective-permute-start(f32[864,128]{1,0:T(8,128)S(1)} %get-tuple-element.112), channel_id=1, source_target_pairs={{0,6},{1,7},{2,4},{3,5},{4,2},{5,3},{6,0},{7,1},{8,14},{9,15},{10,... | collective-permute-start | bytes 1327112 | tf_op jit(solution)/shard_map/cond/branch_0_fun/ppermute | solution.py:432
  108.7 29.2 %collective-permute-start.25 = (f32[864,128]{1,0:T(8,128)S(1)}, f32[864,128]{1,0:T(8,128)S(1)}, u32[]{:S(2)}, u32[]{:S(2)}) collective-permute-start(f32[864,128]{1,0:T(8,128)S(1)} %get-tuple-element.113), channel_id=1, source_target_pairs={{0,7},{1,6},{2,5},{3,4},{4,3},{5,2},{6,1},{7,0},{8,15},{9,14},{10,... | collective-permute-start | bytes 1327112 | tf_op jit(solution)/shard_map/cond/branch_0_fun/ppermute | solution.py:432
  139.2 2.2 %collective-permute-start.26 = (f32[4,4]{1,0:T(4,128)S(1)}, f32[4,4]{1,0:T(4,128)S(1)}, u32[]{:S(2)}, u32[]{:S(2)}) collective-permute-start(f32[4,4]{1,0:T(4,128)S(1)} %div.8), channel_id=1, source_target_pairs={{0,1},{1,0},{2,3},{3,2},{4,5},{5,4},{6,7},{7,6},{8,9},{9,8},{10,11... | collective-permute-start | bytes 200 | tf_op jit(solution)/shard_map/cond/branch_0_fun/ppermute | solution.py:432
  141.5 4.5 %collective-permute-start.29 = (f32[4,4]{1,0:T(4,128)S(1)}, f32[4,4]{1,0:T(4,128)S(1)}, u32[]{:S(2)}, u32[]{:S(2)}) collective-permute-start(f32[4,4]{1,0:T(4,128)S(1)} %add.25), channel_id=1, source_target_pairs={{0,6},{1,7},{2,4},{3,5},{4,2},{5,3},{6,0},{7,1},{8,14},{9,15},{10,... | collective-permute-start | bytes 200 | tf_op jit(solution)/shard_map/cond/branch_0_fun/ppermute | solution.py:432
  143.0 3.6 %collective-permute-start.28 = (f32[4,4]{1,0:T(4,128)S(1)}, f32[4,4]{1,0:T(4,128)S(1)}, u32[]{:S(2)}, u32[]{:S(2)}) collective-permute-start(f32[4,4]{1,0:T(4,128)S(1)} %add.25), channel_id=1, source_target_pairs={{0,4},{1,5},{2,6},{3,7},{4,0},{5,1},{6,2},{7,3},{8,12},{9,13},{10,... | collective-permute-start | bytes 200 | tf_op jit(solution)/shard_map/cond/branch_0_fun/ppermute | solution.py:432
  143.6 3.6 %collective-permute-start.27 = (f32[4,4]{1,0:T(4,128)S(1)}, f32[4,4]{1,0:T(4,128)S(1)}, u32[]{:S(2)}, u32[]{:S(2)}) collective-permute-start(f32[4,4]{1,0:T(4,128)S(1)} %add.25), channel_id=1, source_target_pairs={{0,2},{1,3},{2,0},{3,1},{4,6},{5,7},{6,4},{7,5},{8,10},{9,11},{10,... | collective-permute-start | bytes 200 | tf_op jit(solution)/shard_map/cond/branch_0_fun/ppermute | solution.py:432
  147.2 1.2 copy-start.3
  147.2 1.2 copy-start.9
where the time goes:
time: 150 us; the launch traced here: 148 us
  waiting for transfers between devices  82.6 us (55%)
  starting transfers between devices  32 us (21%)
  Pallas kernels  29.1 us (19%)
  local copies, waits for them, and re-layouts  2.87 us (2%)
    ppermute x26, waiting for transfers between devices, to_partner(): return lax.ppermute(block, 'grid', [(i, i ^ flip) for i in range(SLABS)])  70.8 us
    pallas_call x2, Pallas kernels, pair_step(): pl.pallas_call(functools.partial(pair_kernel, turn), out_shape=[slab] * S...  23.1 us
    ppermute x26, starting transfers between devices, to_partner(): return lax.ppermute(block, 'grid', [(i, i ^ flip) for i in range(SLABS)])  20 us
    ppermute x4, starting transfers between devices, to_group(): return lax.ppermute(block, ('band', 'grid'), route)  12 us
    ppermute x4, waiting for transfers between devices, to_group(): return lax.ppermute(block, ('band', 'grid'), route)  11.8 us
  transfers between devices with their start and end apart: 30, of which 14 were waited for; matrix products, arithmetic and copies ran while one was open for 0% of the time, Pallas kernels for 10%

commit v1 on v0

--- a/solution.py
+++ b/solution.py
@@ -368,7 +368,7 @@
         out_specs=[in_vmem] * SLABS if turn else in_vmem,
         scratch_shapes=[
             pltpu.VMEM((COLS, NX, LANES), f32),
-            pltpu.VMEM((NY * PITCH, LANES), f32),
+            pltpu.VMEM((NY * PITCH + NX, LANES), f32),
         ],
         compiler_params=pltpu.CompilerParams(vmem_limit_bytes=PAIR_VMEM),
         cost_estimate=pl.CostEstimate(flops=0, bytes_accessed=1 << 20, transcendentals=0),

time: 150 us -> 183 us (1.22)
  waiting for transfers between devices: 82.6 us -> 128 us
  starting transfers between devices: 32 us -> 20.5 us
    ppermute x4, waiting for transfers between devices: 11.8 us -> 64.6 us  [to_group(): return lax.ppermute(block, ('band', 'grid'), route)]
    ppermute x4, starting transfers between devices: 12 us -> 2.94 us  [to_group(): return lax.ppermute(block, ('band', 'grid'), route)]
    ppermute x26, waiting for transfers between devices: 70.8 us -> 63.3 us  [to_partner(): return lax.ppermute(block, 'grid', [(i, i ^ flip) for i in range(SLABS)])]
    ppermute x26, starting transfers between devices: 20 us -> 17.5 us  [to_partner(): return lax.ppermute(block, 'grid', [(i, i ^ flip) for i in range(SLABS)])]
  transfers between devices with their start and end apart: 30 -> 30, of which waited for: 14 -> 13; matrix products, arithmetic and copies ran while one was open for 0% -> 0% of each run, Pallas kernels for 10% -> 8%
where the time goes in v1:
time: 183 us; the launch traced here: 182 us
  waiting for transfers between devices  128 us (70%)
  Pallas kernels  29.1 us (16%)
  starting transfers between devices  20.5 us (11%)
  local copies, waits for them, and re-layouts  2.86 us (2%)
    ppermute x4, waiting for transfers between devices, to_group(): return lax.ppermute(block, ('band', 'grid'), route)  64.6 us
    ppermute x26, waiting for transfers between devices, to_partner(): return lax.ppermute(block, 'grid', [(i, i ^ flip) for i in range(SLABS)])  63.3 us
    pallas_call x2, Pallas kernels, pair_step(): pl.pallas_call(functools.partial(pair_kernel, turn), out_shape=[slab] * S...  23.1 us
    ppermute x26, starting transfers between devices, to_partner(): return lax.ppermute(block, 'grid', [(i, i ^ flip) for i in range(SLABS)])  17.5 us
  transfers between devices with their start and end apart: 30, of which 13 were waited for; matrix products, arithmetic and copies ran while one was open for 0% of the time, Pallas kernels for 8%

profile of v1, /device:TPU:0, one launch (start us, length us, event | category | flops | bytes accessed | tf_op | source)
XLA Modules:
  0.0 182.3 jit_solution(15869749604882922686)
XLA Ops:
  1.3 1.5 copy-done
  2.8 1.5 shard_map.86
  4.3 176.8 %conditional.1 = (f32[12,4,9216]{2,1,0:T(4,128)S(1)}, f32[4,4]{1,0:T(4,128)S(1)}) conditional(s32[]{:T(128)} %clamp.3, (f32[2,864,128]{2,1,0:T(8,128)S(1)}, f32[1,864,128]{2,1,0:T(8,128)S(1)}, f32[1,864,128]{2,1,0:T(8,128)S(1)}, f32[1,864,128]{2,1,0:T(8,128)S(1)}, f32[1,864,128]{2,1,0:T(8,128)S(1)}, ...), branch_computations={%region_0.0_spmd, %region_2.0_spmd, %region_4.0_spmd} | conditional | flops 665664 | bytes 85699616 | solution.py:491
  4.5 3.0 %collective-permute-start.30 = (f32[2,864,128]{2,1,0:T(8,128)S(1)}, f32[2,864,128]{2,1,0:T(8,128)S(1)}, u32[]{:S(2)}, u32[]{:S(2)}) collective-permute-start(f32[2,864,128]{2,1,0:T(8,128)S(1)} %get-tuple-element.119.refs_10_), channel_id=1, source_target_pairs={{0,2},{1,3},{2,0},{3,1},{4,6},{5,7},{6,4},{7,5},{8,10},{9,11},{10,... | collective-permute-start | bytes 2654216 | tf_op jit(solution)/shard_map/cond/branch_1_fun/ppermute | solution.py:432
  7.6 2.6 %collective-permute-start.33 = (f32[1,864,128]{2,1,0:T(8,128)S(1)}, f32[1,864,128]{2,1,0:T(8,128)S(1)}, u32[]{:S(2)}, u32[]{:S(2)}) collective-permute-start(f32[1,864,128]{2,1,0:T(8,128)S(1)} %get-tuple-element.121), channel_id=1, source_target_pairs={{0,16},{1,17},{2,18},{3,19},{4,20},{5,21},{6,22},{7,23},{8,24},{9,... | collective-permute-start | bytes 1327112 | tf_op jit(solution)/shard_map/cond/branch_1_fun/ppermute | solution.py:438
  10.1 1.5 collective-permute-start.31
  11.7 0.3 collective-permute-start.34
  11.9 1.5 collective-permute-start.32
  13.5 26.7 %collective-permute-done.33 = f32[1,864,128]{2,1,0:T(8,128)S(1)} collective-permute-done((f32[1,864,128]{2,1,0:T(8,128)S(1)}, f32[1,864,128]{2,1,0:T(8,128)S(1)}, u32[]{:S(2)}, u32[]{:S(2)}) %collective-permute-start.33) | collective-permute-done | bytes 442400 | tf_op jit(solution)/shard_map/cond/branch_1_fun/ppermute | solution.py:438
  40.2 9.2 %collective-permute-done.34 = f32[1,864,128]{2,1,0:T(8,128)S(1)} collective-permute-done((f32[1,864,128]{2,1,0:T(8,128)S(1)}, f32[1,864,128]{2,1,0:T(8,128)S(1)}, u32[]{:S(2)}, u32[]{:S(2)}) %collective-permute-start.34) | collective-permute-done | bytes 442400 | tf_op jit(solution)/shard_map/cond/branch_1_fun/ppermute | solution.py:438
  49.6 0.6 collective-permute-start.42
  50.2 1.5 branch_1_fun.5
  51.7 0.5 collective-permute-start.35
  52.3 19.7 %collective-permute-done.36.refs_10_ = f32[1,864,128]{2,1,0:T(8,128)S(1)} collective-permute-done((f32[1,864,128]{2,1,0:T(8,128)S(1)}, f32[1,864,128]{2,1,0:T(8,128)S(1)}, u32[]{:S(2)}, u32[]{:S(2)}) %collective-permute-start.36) | collective-permute-done | bytes 442400 | tf_op jit(solution)/shard_map/cond/branch_1_fun/ppermute | solution.py:438
  72.0 0.1 pad_maximum_fusion.1
  72.1 0.1 collective-permute-start.37
  72.1 0.5 collective-permute-start.41
  72.6 0.1 collective-permute-start.43
  72.7 8.6 %collective-permute-done.35.refs_3_ = f32[2,864,128]{2,1,0:T(8,128)S(1)} collective-permute-done((f32[2,864,128]{2,1,0:T(8,128)S(1)}, f32[2,864,128]{2,1,0:T(8,128)S(1)}, u32[]{:S(2)}, u32[]{:S(2)}) %collective-permute-start.35) | collective-permute-done | bytes 884768 | tf_op jit(solution)/shard_map/cond/branch_1_fun/ppermute | solution.py:432
  81.4 0.6 collective-permute-start.47
  82.0 1.8 collective-permute-done.38.refs_5_
  83.8 11.6 %branch_1_fun.6.refs_19_ = f32[72,96,128]{2,1,0:T(8,128)S(1)} custom-call(s32[1]{0:T(128)} %get-tuple-element.124.place, s32[4,4]{1,0:T(4,128)S(1)} %get-tuple-element.117.mask, f32[1,864,128]{2,1,0:T(8,128)S(1)} %get-tuple-element.118.refs_0_.refs_8_, f32[2,864,128]{2,1,0:T(8,128)S(1)} %collective-permute-done.30.refs_1_, ...), custom_call_target="tpu_custom_call" | custom-call | bytes 1048576 | tf_op jit(solution)/shard_map/cond/branch_1_fun/pallas_call | solution.py:364
  95.3 9.0 %collective-permute-done.39.refs_6_ = f32[1,864,128]{2,1,0:T(8,128)S(1)} collective-permute-done((f32[1,864,128]{2,1,0:T(8,128)S(1)}, f32[1,864,128]{2,1,0:T(8,128)S(1)}, u32[]{:S(2)}, u32[]{:S(2)}) %collective-permute-start.39) | collective-permute-done | bytes 442400 | tf_op jit(solution)/shard_map/cond/branch_1_fun/ppermute | solution.py:438
  104.3 0.6 collective-permute-start.44
  104.9 0.5 collective-permute-start.40
  105.4 10.7 %collective-permute-done.44.refs_8_ = f32[1,864,128]{2,1,0:T(8,128)S(1)} collective-permute-done((f32[1,864,128]{2,1,0:T(8,128)S(1)}, f32[1,864,128]{2,1,0:T(8,128)S(1)}, u32[]{:S(2)}, u32[]{:S(2)}) %collective-permute-start.44) | collective-permute-done | bytes 442400 | tf_op jit(solution)/shard_map/cond/branch_1_fun/ppermute | solution.py:432
  116.1 1.8 collective-permute-done.45.refs_9_
  117.9 11.6 %branch_1_fun.7 = (f32[864,128]{1,0:T(8,128)S(1)}, f32[864,128]{1,0:T(8,128)S(1)}, f32[864,128]{1,0:T(8,128)S(1)}, f32[864,128]{1,0:T(8,128)S(1)}, f32[864,128]{...) custom-call(s32[1]{0:T(128)} %get-tuple-element.124.place, ...), custom_call_target="tpu_custom_call" | custom-call | bytes 1048576 | tf_op jit(solution)/shard_map/cond/branch_1_fun/pallas_call | solution.py:364
  129.5 0.2 collective-permute-start.49
  129.7 0.6 collective-permute-start.50
  130.3 1.2 collective-permute-start.51
  131.4 0.5 collective-permute-start.52
  131.9 1.3 collective-permute-start.53
  133.2 0.5 collective-permute-start.54
  133.7 9.0 %collective-permute-done.50.refs_2_ = f32[864,128]{1,0:T(8,128)S(1)} collective-permute-done((f32[864,128]{1,0:T(8,128)S(1)}, f32[864,128]{1,0:T(8,128)S(1)}, u32[]{:S(2)}, u32[]{:S(2)}) %collective-permute-start.50) | collective-permute-done | bytes 442400 | tf_op jit(solution)/shard_map/cond/branch_1_fun/ppermute | solution.py:432
  142.7 8.4 %collective-permute-done.51.refs_3_ = f32[864,128]{1,0:T(8,128)S(1)} collective-permute-done((f32[864,128]{1,0:T(8,128)S(1)}, f32[864,128]{1,0:T(8,128)S(1)}, u32[]{:S(2)}, u32[]{:S(2)}) %collective-permute-start.51) | collective-permute-done | bytes 442400 | tf_op jit(solution)/shard_map/cond/branch_1_fun/ppermute | solution.py:432
  151.1 20.9 %collective-permute-done.53.refs_5_ = f32[864,128]{1,0:T(8,128)S(1)} collective-permute-done((f32[864,128]{1,0:T(8,128)S(1)}, f32[864,128]{1,0:T(8,128)S(1)}, u32[]{:S(2)}, u32[]{:S(2)}) %collective-permute-start.53) | collective-permute-done | bytes 442400 | tf_op jit(solution)/shard_map/cond/branch_1_fun/ppermute | solution.py:432
  171.9 1.0 branch_1_fun.8
  172.9 0.2 reduce_sum.25
  173.1 0.1 div.12
  173.2 0.3 collective-permute-start.56
  173.5 1.9 %branch_1_fun.9 = f32[12,4,9216]{2,1,0:T(4,128)S(1)} custom-call(f32[4,864,128]{2,1,0:T(8,128)S(1)} %get-tuple-element.153.natural), custom_call_target="tpu_custom_call" | custom-call | bytes 8388608 | tf_op jit(solution)/shard_map/cond/branch_1_fun/pallas_call | solution.py:417
  175.5 0.5 collective-permute-start.59
  176.0 1.6 collective-permute-start.58
  177.5 1.5 collective-permute-start.57
  179.0 1.0 collective-permute-done.59
  180.0 1.1 collective-permute-done.57
  181.2 1.2 copy-done.3
  (44 shorter events, 0.3 us)
Async XLA Ops:
  0.6 3.7 %copy-start.8 = (s32[4,4]{1,0:T(4,128)S(1)}, s32[4,4]{1,0:T(4,128)}, u32[]{:S(2)}) copy-start(s32[4,4]{1,0:T(4,128)} %param.11) | copy-start | bytes 196
  1.3 1.5 copy-start
  2.8 1.5 copy-start.1
  2.8 1.5 copy-start.2
  2.8 1.5 copy-start.4
  4.5 45.7 %copy-start.6 = (bf16[192,192]{1,0:T(8,128)(2,1)S(1)}, bf16[192,192]{1,0:T(8,128)(2,1)}, u32[]{:S(2)}) copy-start(bf16[192,192]{1,0:T(8,128)(2,1)} %get-tuple-element.126.rows_in) | copy-start | bytes 221188 | tf_op jit(solution)/shard_map/cond
  4.5 35.7 %collective-permute-start.30 = (f32[2,864,128]{2,1,0:T(8,128)S(1)}, f32[2,864,128]{2,1,0:T(8,128)S(1)}, u32[]{:S(2)}, u32[]{:S(2)}) collective-permute-start(f32[2,864,128]{2,1,0:T(8,128)S(1)} %get-tuple-element.119.refs_10_), channel_id=1, source_target_pairs={{0,2},{1,3},{2,0},{3,1},{4,6},{5,7},{6,4},{7,5},{8,10},{9,11},{10,... | collective-permute-start | bytes 2654216 | tf_op jit(solution)/shard_map/cond/branch_1_fun/ppermute | solution.py:432
  7.6 32.6 %collective-permute-start.33 = (f32[1,864,128]{2,1,0:T(8,128)S(1)}, f32[1,864,128]{2,1,0:T(8,128)S(1)}, u32[]{:S(2)}, u32[]{:S(2)}) collective-permute-start(f32[1,864,128]{2,1,0:T(8,128)S(1)} %get-tuple-element.121), channel_id=1, source_target_pairs={{0,16},{1,17},{2,18},{3,19},{4,20},{5,21},{6,22},{7,23},{8,24},{9,... | collective-permute-start | bytes 1327112 | tf_op jit(solution)/shard_map/cond/branch_1_fun/ppermute | solution.py:438
  10.1 30.1 %collective-permute-start.31 = (f32[1,864,128]{2,1,0:T(8,128)S(1)}, f32[1,864,128]{2,1,0:T(8,128)S(1)}, u32[]{:S(2)}, u32[]{:S(2)}) collective-permute-start(f32[1,864,128]{2,1,0:T(8,128)S(1)} %get-tuple-element.118.refs_0_.refs_8_), channel_id=1, source_target_pairs={{0,4},{1,5},{2,6},{3,7},{4,0},{5,1},{6,2},{7,3},{8,12},{9,13},{10,... | collective-permute-start | bytes 1327112 | tf_op jit(solution)/shard_map/cond/branch_1_fun/ppermute | solution.py:432
  11.7 37.8 %collective-permute-start.34 = (f32[1,864,128]{2,1,0:T(8,128)S(1)}, f32[1,864,128]{2,1,0:T(8,128)S(1)}, u32[]{:S(2)}, u32[]{:S(2)}) collective-permute-start(f32[1,864,128]{2,1,0:T(8,128)S(1)} %get-tuple-element.123), channel_id=1, source_target_pairs={{0,20},{1,21},{2,22},{3,23},{4,16},{5,17},{6,18},{7,19},{8,28},{9,... | collective-permute-start | bytes 1327112 | tf_op jit(solution)/shard_map/cond/branch_1_fun/ppermute | solution.py:438
  11.9 39.8 %collective-permute-start.32 = (f32[1,864,128]{2,1,0:T(8,128)S(1)}, f32[1,864,128]{2,1,0:T(8,128)S(1)}, u32[]{:S(2)}, u32[]{:S(2)}) collective-permute-start(f32[1,864,128]{2,1,0:T(8,128)S(1)} %get-tuple-element.137.refs_9_), channel_id=1, source_target_pairs={{0,4},{1,5},{2,6},{3,7},{4,0},{5,1},{6,2},{7,3},{8,12},{9,13},{10,... | collective-permute-start | bytes 1327112 | tf_op jit(solution)/shard_map/cond/branch_1_fun/ppermute | solution.py:432
  49.5 22.5 %collective-permute-start.36 = (f32[1,864,128]{2,1,0:T(8,128)S(1)}, f32[1,864,128]{2,1,0:T(8,128)S(1)}, u32[]{:S(2)}, u32[]{:S(2)}) collective-permute-start(f32[1,864,128]{2,1,0:T(8,128)S(1)} %get-tuple-element.136), channel_id=1, source_target_pairs={{0,20},{1,21},{2,22},{3,23},{4,16},{5,17},{6,18},{7,19},{8,28},{9,... | collective-permute-start | bytes 1327112 | tf_op jit(solution)/shard_map/cond/branch_1_fun/ppermute | solution.py:438
  49.6 23.1 %collective-permute-start.42 = (f32[2,864,128]{2,1,0:T(8,128)S(1)}, f32[2,864,128]{2,1,0:T(8,128)S(1)}, u32[]{:S(2)}, u32[]{:S(2)}) collective-permute-start(f32[2,864,128]{2,1,0:T(8,128)S(1)} %constant_dynamic-update-slice_fusion.2.refs_6_), channel_id=1, source_target_pairs={{0,2},{1,3},{2,0},{3,1},{4,6},{5,7},{6,4},{7,5},{8,10},{9,11},{10,... | collective-permute-start | bytes 2654216 | tf_op jit(solution)/shard_map/cond/branch_1_fun/ppermute | solution.py:432
  51.7 29.6 %collective-permute-start.35 = (f32[2,864,128]{2,1,0:T(8,128)S(1)}, f32[2,864,128]{2,1,0:T(8,128)S(1)}, u32[]{:S(2)}, u32[]{:S(2)}) collective-permute-start(f32[2,864,128]{2,1,0:T(8,128)S(1)} %collective-permute-done.30.refs_1_), channel_id=1, source_target_pairs={{0,4},{1,5},{2,6},{3,7},{4,0},{5,1},{6,2},{7,3},{8,12},{9,13},{10,... | collective-permute-start | bytes 2654216 | tf_op jit(solution)/shard_map/cond/branch_1_fun/ppermute | solution.py:432
  72.1 9.9 %collective-permute-start.37 = (f32[3,864,128]{2,1,0:T(8,128)S(1)}, f32[3,864,128]{2,1,0:T(8,128)S(1)}, u32[]{:S(2)}, u32[]{:S(2)}) collective-permute-start(f32[3,864,128]{2,1,0:T(8,128)S(1)} %pad_maximum_fusion.1), channel_id=1, source_target_pairs={{0,1},{1,0},{2,3},{3,2},{4,5},{5,4},{6,7},{7,6},{8,9},{9,8},{10,11... | collective-permute-start | bytes 3981320 | tf_op jit(solution)/shard_map/cond/branch_1_fun/ppermute | solution.py:432
  72.1 9.2 %collective-permute-start.41 = (f32[2,864,128]{2,1,0:T(8,128)S(1)}, f32[2,864,128]{2,1,0:T(8,128)S(1)}, u32[]{:S(2)}, u32[]{:S(2)}) collective-permute-start(f32[2,864,128]{2,1,0:T(8,128)S(1)} %constant_dynamic-update-slice_fusion.2.refs_6_), channel_id=1, source_target_pairs={{0,1},{1,0},{2,3},{3,2},{4,5},{5,4},{6,7},{7,6},{8,9},{9,8},{10,11... | collective-permute-start | bytes 2654216 | tf_op jit(solution)/shard_map/cond/branch_1_fun/ppermute | solution.py:432
  72.6 9.3 %collective-permute-start.43 = (f32[2,864,128]{2,1,0:T(8,128)S(1)}, f32[2,864,128]{2,1,0:T(8,128)S(1)}, u32[]{:S(2)}, u32[]{:S(2)}) collective-permute-start(f32[2,864,128]{2,1,0:T(8,128)S(1)} %collective-permute-done.42.refs_8_), channel_id=1, source_target_pairs={{0,1},{1,0},{2,3},{3,2},{4,5},{5,4},{6,7},{7,6},{8,9},{9,8},{10,11... | collective-permute-start | bytes 2654216 | tf_op jit(solution)/shard_map/cond/branch_1_fun/ppermute | solution.py:432
  81.4 2.4 %collective-permute-start.38 = (f32[2,864,128]{2,1,0:T(8,128)S(1)}, f32[2,864,128]{2,1,0:T(8,128)S(1)}, u32[]{:S(2)}, u32[]{:S(2)}) collective-permute-start(f32[2,864,128]{2,1,0:T(8,128)S(1)} %collective-permute-done.35.refs_3_), channel_id=1, source_target_pairs={{0,1},{1,0},{2,3},{3,2},{4,5},{5,4},{6,7},{7,6},{8,9},{9,8},{10,11... | collective-permute-start | bytes 2654216 | tf_op jit(solution)/shard_map/cond/branch_1_fun/ppermute | solution.py:432
  81.4 23.0 %collective-permute-start.39 = (f32[1,864,128]{2,1,0:T(8,128)S(1)}, f32[1,864,128]{2,1,0:T(8,128)S(1)}, u32[]{:S(2)}, u32[]{:S(2)}) collective-permute-start(f32[1,864,128]{2,1,0:T(8,128)S(1)} %get-tuple-element.140), channel_id=1, source_target_pairs={{0,16},{1,17},{2,18},{3,19},{4,20},{5,21},{6,22},{7,23},{8,24},{9,... | collective-permute-start | bytes 1327112 | tf_op jit(solution)/shard_map/cond/branch_1_fun/ppermute | solution.py:438
  81.4 24.0 %collective-permute-start.47 = (f32[1,864,128]{2,1,0:T(8,128)S(1)}, f32[1,864,128]{2,1,0:T(8,128)S(1)}, u32[]{:S(2)}, u32[]{:S(2)}) collective-permute-start(f32[1,864,128]{2,1,0:T(8,128)S(1)} %collective-permute-done.36.refs_10_), channel_id=1, source_target_pairs={{0,2},{1,3},{2,0},{3,1},{4,6},{5,7},{6,4},{7,5},{8,10},{9,11},{10,... | collective-permute-start | bytes 1327112 | tf_op jit(solution)/shard_map/cond/branch_1_fun/ppermute | solution.py:432
  104.3 11.8 %collective-permute-start.44 = (f32[1,864,128]{2,1,0:T(8,128)S(1)}, f32[1,864,128]{2,1,0:T(8,128)S(1)}, u32[]{:S(2)}, u32[]{:S(2)}) collective-permute-start(f32[1,864,128]{2,1,0:T(8,128)S(1)} %collective-permute-done.39.refs_6_), channel_id=1, source_target_pairs={{0,2},{1,3},{2,0},{3,1},{4,6},{5,7},{6,4},{7,5},{8,10},{9,11},{10,... | collective-permute-start | bytes 1327112 | tf_op jit(solution)/shard_map/cond/branch_1_fun/ppermute | solution.py:432
  104.9 11.3 %collective-permute-start.46 = (f32[1,864,128]{2,1,0:T(8,128)S(1)}, f32[1,864,128]{2,1,0:T(8,128)S(1)}, u32[]{:S(2)}, u32[]{:S(2)}) collective-permute-start(f32[1,864,128]{2,1,0:T(8,128)S(1)} %collective-permute-done.36.refs_10_), channel_id=1, source_target_pairs={{0,1},{1,0},{2,3},{3,2},{4,5},{5,4},{6,7},{7,6},{8,9},{9,8},{10,11... | collective-permute-start | bytes 1327112 | tf_op jit(solution)/shard_map/cond/branch_1_fun/ppermute | solution.py:432
  104.9 11.3 %collective-permute-start.40 = (f32[1,864,128]{2,1,0:T(8,128)S(1)}, f32[1,864,128]{2,1,0:T(8,128)S(1)}, u32[]{:S(2)}, u32[]{:S(2)}) collective-permute-start(f32[1,864,128]{2,1,0:T(8,128)S(1)} %collective-permute-done.39.refs_6_), channel_id=1, source_target_pairs={{0,1},{1,0},{2,3},{3,2},{4,5},{5,4},{6,7},{7,6},{8,9},{9,8},{10,11... | collective-permute-start | bytes 1327112 | tf_op jit(solution)/shard_map/cond/branch_1_fun/ppermute | solution.py:432
  105.4 10.7 %collective-permute-start.48 = (f32[1,864,128]{2,1,0:T(8,128)S(1)}, f32[1,864,128]{2,1,0:T(8,128)S(1)}, u32[]{:S(2)}, u32[]{:S(2)}) collective-permute-start(f32[1,864,128]{2,1,0:T(8,128)S(1)} %collective-permute-done.47.refs_12_), channel_id=1, source_target_pairs={{0,1},{1,0},{2,3},{3,2},{4,5},{5,4},{6,7},{7,6},{8,9},{9,8},{10,11... | collective-permute-start | bytes 1327112 | tf_op jit(solution)/shard_map/cond/branch_1_fun/ppermute | solution.py:432
  116.1 1.8 collective-permute-start.45
  129.5 3.7 %collective-permute-start.49 = (f32[864,128]{1,0:T(8,128)S(1)}, f32[864,128]{1,0:T(8,128)S(1)}, u32[]{:S(2)}, u32[]{:S(2)}) collective-permute-start(f32[864,128]{1,0:T(8,128)S(1)} %get-tuple-element.146), channel_id=1, source_target_pairs={{0,1},{1,0},{2,3},{3,2},{4,5},{5,4},{6,7},{7,6},{8,9},{9,8},{10,11... | collective-permute-start | bytes 1327112 | tf_op jit(solution)/shard_map/cond/branch_1_fun/ppermute | solution.py:432
  129.7 13.0 %collective-permute-start.50 = (f32[864,128]{1,0:T(8,128)S(1)}, f32[864,128]{1,0:T(8,128)S(1)}, u32[]{:S(2)}, u32[]{:S(2)}) collective-permute-start(f32[864,128]{1,0:T(8,128)S(1)} %get-tuple-element.147), channel_id=1, source_target_pairs={{0,2},{1,3},{2,0},{3,1},{4,6},{5,7},{6,4},{7,5},{8,10},{9,11},{10,... | collective-permute-start | bytes 1327112 | tf_op jit(solution)/shard_map/cond/branch_1_fun/ppermute | solution.py:432
  130.3 20.8 %collective-permute-start.51 = (f32[864,128]{1,0:T(8,128)S(1)}, f32[864,128]{1,0:T(8,128)S(1)}, u32[]{:S(2)}, u32[]{:S(2)}) collective-permute-start(f32[864,128]{1,0:T(8,128)S(1)} %get-tuple-element.148), channel_id=1, source_target_pairs={{0,3},{1,2},{2,1},{3,0},{4,7},{5,6},{6,5},{7,4},{8,11},{9,10},{10,... | collective-permute-start | bytes 1327112 | tf_op jit(solution)/shard_map/cond/branch_1_fun/ppermute | solution.py:432
  131.4 19.6 %collective-permute-start.52 = (f32[864,128]{1,0:T(8,128)S(1)}, f32[864,128]{1,0:T(8,128)S(1)}, u32[]{:S(2)}, u32[]{:S(2)}) collective-permute-start(f32[864,128]{1,0:T(8,128)S(1)} %get-tuple-element.149), channel_id=1, source_target_pairs={{0,4},{1,5},{2,6},{3,7},{4,0},{5,1},{6,2},{7,3},{8,12},{9,13},{10,... | collective-permute-start | bytes 1327112 | tf_op jit(solution)/shard_map/cond/branch_1_fun/ppermute | solution.py:432
  131.9 40.0 %collective-permute-start.53 = (f32[864,128]{1,0:T(8,128)S(1)}, f32[864,128]{1,0:T(8,128)S(1)}, u32[]{:S(2)}, u32[]{:S(2)}) collective-permute-start(f32[864,128]{1,0:T(8,128)S(1)} %get-tuple-element.150), channel_id=1, source_target_pairs={{0,5},{1,4},{2,7},{3,6},{4,1},{5,0},{6,3},{7,2},{8,13},{9,12},{10,... | collective-permute-start | bytes 1327112 | tf_op jit(solution)/shard_map/cond/branch_1_fun/ppermute | solution.py:432
  133.2 38.7 %collective-permute-start.54 = (f32[864,128]{1,0:T(8,128)S(1)}, f32[864,128]{1,0:T(8,128)S(1)}, u32[]{:S(2)}, u32[]{:S(2)}) collective-permute-start(f32[864,128]{1,0:T(8,128)S(1)} %get-tuple-element.151), channel_id=1, source_target_pairs={{0,6},{1,7},{2,4},{3,5},{4,2},{5,3},{6,0},{7,1},{8,14},{9,15},{10,... | collective-permute-start | bytes 1327112 | tf_op jit(solution)/shard_map/cond/branch_1_fun/ppermute | solution.py:432
  142.7 29.2 %collective-permute-start.55 = (f32[864,128]{1,0:T(8,128)S(1)}, f32[864,128]{1,0:T(8,128)S(1)}, u32[]{:S(2)}, u32[]{:S(2)}) collective-permute-start(f32[864,128]{1,0:T(8,128)S(1)} %get-tuple-element.152), channel_id=1, source_target_pairs={{0,7},{1,6},{2,5},{3,4},{4,3},{5,2},{6,1},{7,0},{8,15},{9,14},{10,... | collective-permute-start | bytes 1327112 | tf_op jit(solution)/shard_map/cond/branch_1_fun/ppermute | solution.py:432
  173.2 2.2 %collective-permute-start.56 = (f32[4,4]{1,0:T(4,128)S(1)}, f32[4,4]{1,0:T(4,128)S(1)}, u32[]{:S(2)}, u32[]{:S(2)}) collective-permute-start(f32[4,4]{1,0:T(4,128)S(1)} %div.12), channel_id=1, source_target_pairs={{0,1},{1,0},{2,3},{3,2},{4,5},{5,4},{6,7},{7,6},{8,9},{9,8},{10,11... | collective-permute-start | bytes 200 | tf_op jit(solution)/shard_map/cond/branch_1_fun/ppermute | solution.py:432
  175.5 4.5 %collective-permute-start.59 = (f32[4,4]{1,0:T(4,128)S(1)}, f32[4,4]{1,0:T(4,128)S(1)}, u32[]{:S(2)}, u32[]{:S(2)}) collective-permute-start(f32[4,4]{1,0:T(4,128)S(1)} %add.29), channel_id=1, source_target_pairs={{0,6},{1,7},{2,4},{3,5},{4,2},{5,3},{6,0},{7,1},{8,14},{9,15},{10,... | collective-permute-start | bytes 200 | tf_op jit(solution)/shard_map/cond/branch_1_fun/ppermute | solution.py:432
  176.0 4.0 %collective-permute-start.58 = (f32[4,4]{1,0:T(4,128)S(1)}, f32[4,4]{1,0:T(4,128)S(1)}, u32[]{:S(2)}, u32[]{:S(2)}) collective-permute-start(f32[4,4]{1,0:T(4,128)S(1)} %add.29), channel_id=1, source_target_pairs={{0,4},{1,5},{2,6},{3,7},{4,0},{5,1},{6,2},{7,3},{8,12},{9,13},{10,... | collective-permute-start | bytes 200 | tf_op jit(solution)/shard_map/cond/branch_1_fun/ppermute | solution.py:432
  177.5 3.6 %collective-permute-start.57 = (f32[4,4]{1,0:T(4,128)S(1)}, f32[4,4]{1,0:T(4,128)S(1)}, u32[]{:S(2)}, u32[]{:S(2)}) collective-permute-start(f32[4,4]{1,0:T(4,128)S(1)} %add.29), channel_id=1, source_target_pairs={{0,2},{1,3},{2,0},{3,1},{4,6},{5,7},{6,4},{7,5},{8,10},{9,11},{10,... | collective-permute-start | bytes 200 | tf_op jit(solution)/shard_map/cond/branch_1_fun/ppermute | solution.py:432
  181.1 1.2 copy-start.3
  181.1 1.2 copy-start.9
